TPU v7x, 32 devices: a whole 2x2x4 slice. The times are simulated.
32 devices in a mesh: rows: 16 (over z, y, x), grp: 2 (over core).
Axes of the slice: x: 2, y: 2, z: 4, core: 2. Of those that a mesh axis runs over, the one named last changes fastest.
Arguments:
- snap_early: float32 [3072, 128, 128], P(('rows', 'grp')), as said below
- snap_late: float32 [3072, 128, 128], P(('rows', 'grp')), as said below
- block_ids: int32 [3072], P(('rows', 'grp')), may hold values from 0 to 3071, as said below
- block_owner: int32 [3072], replicated, may hold values from 0 to 31, as said below
- block_slot: int32 [3072], replicated, may hold values from 0 to 127, as said below
Outputs:
- modes: float32 [4096, 128, 128], P(('rows', 'grp'))
- operator: float32 [128, 128], replicated
Inputs may be any that keep to these rules, and one draw needn't show every extreme that they name: block_ids is a permutation of 0 to 3071. `block_owner`: each analysis device owns at most 128 blocks and one owns exactly 128; among the blocks of one solver device (aligned runs of 96 slots of block_ids) at most 4 go to one analysis device, and in every draw some solver device sends exactly 4 to one. `block_slot`: the blocks of one analysis device take the slots 0 to c - 1, each once, where c is their count. `snap_early`: Real-valued snapshots with magnitudes from below one to some thousands, row and column scales spread by up to a factor of about 900; the matrix of all rows has full column rank. `snap_late`: Real-valued snapshots, the early ones advanced by one step of a linear flow plus noise.
All inputs are finite; a program needn't handle non-finite values.
Results may differ from a plain program's by a relative error of at most 0.0003.
Values sent between devices are 32-bit elements; how exact they have to be, the bound alone decides.
A program may use at most 128 MiB of HBM per device.

v0:
```python
import jax
import jax.numpy as jnp
from jax import lax
from jax.sharding import PartitionSpec as P

CAP = 128


def swapped(value, axis, stride):
    return lax.ppermute(value, axis, [(i, i ^ 1 << stride) for i in range(lax.axis_size(axis))])


def upper_factor(gram_total):
    order = gram_total.shape[0]
    index = jnp.arange(order, dtype=jnp.int32)

    def step(j, factor):
        column = lax.dynamic_slice_in_dim(factor, j, 1, 1)[:, 0]
        grow = lax.dynamic_slice_in_dim(gram_total, j, 1, 0)[0]
        rest = grow - jnp.dot(column, factor, precision=lax.Precision.HIGHEST)
        pivot = jnp.sqrt(jnp.sum(jnp.where(index == j, rest, 0.0)))
        newrow = jnp.where(index >= j, rest / pivot, 0.0)
        picked = (index == j).astype(gram_total.dtype)
        return factor + picked[:, None] * newrow[None, :]

    return lax.fori_loop(0, order, step, jnp.zeros_like(gram_total))


def upper_inverse(factor):
    order = factor.shape[0]
    index = jnp.arange(order, dtype=jnp.int32)

    def step(t, inverse):
        i = order - 1 - t
        frow = lax.dynamic_slice_in_dim(factor, i, 1, 0)[0]
        unit = (index == i).astype(factor.dtype)
        diagonal = jnp.sum(frow * unit)
        newrow = (unit - jnp.dot(frow, inverse, precision=lax.Precision.HIGHEST)) / diagonal
        return inverse + unit[:, None] * newrow[None, :]

    return lax.fori_loop(0, order, step, jnp.zeros_like(factor))


def gram_pair(early_blocks, late_blocks):
    early_rows = early_blocks.reshape((-1, early_blocks.shape[-1]))
    late_rows = late_blocks.reshape((-1, late_blocks.shape[-1]))
    gram_local = jnp.einsum("rk,rl->kl", early_rows, early_rows, precision=lax.Precision.HIGHEST)
    cross_local = jnp.einsum("rk,rl->kl", early_rows, late_rows, precision=lax.Precision.HIGHEST)
    return jnp.stack([gram_local, cross_local])


def combine_stats(stacked):
    members = lax.axis_size(("rows", "grp"))
    for bit_index in range(members.bit_length() - 1):
        stacked = stacked + swapped(stacked, ("rows", "grp"), bit_index)
    return stacked


def finish(stacked, row_total):
    gram_total = stacked[0] / row_total
    cross_total = stacked[1] / row_total
    inverse = upper_inverse(upper_factor(gram_total))
    coupled = jnp.dot(cross_total, inverse, precision=lax.Precision.HIGHEST)
    operator = jnp.dot(inverse.T, coupled, precision=lax.Precision.HIGHEST)
    return (inverse, operator)


def apply_inverse(late_blocks, inverse):
    late_rows = late_blocks.reshape((-1, late_blocks.shape[-1]))
    solved = jnp.dot(late_rows, inverse, precision=lax.Precision.HIGHEST)
    return solved.reshape(late_blocks.shape)


def select_rows(matches, member):
    flat = member.reshape((member.shape[0], -1))
    chosen = jnp.dot(matches.astype(member.dtype), flat, precision=lax.Precision.HIGHEST)
    return chosen.reshape((matches.shape[0],) + member.shape[1:])


def arrange(values, destination, slot_here, slot_count):
    target = jnp.arange(slot_count, dtype=jnp.int32)
    matches = destination[None, :] == target[:, None]
    usable = jnp.any(matches, axis=1)
    picked = tuple((select_rows(matches, member) for member in values))
    carried = jnp.sum(jnp.where(matches, slot_here[None, :], 0), axis=1)
    slot_sent = jnp.where(usable, carried, -1)
    return picked + (slot_sent,)


def settle(values, slot_arrived, slot_count):
    target = jnp.arange(slot_count, dtype=jnp.int32)
    matches = slot_arrived[None, :] == target[:, None]
    return tuple((select_rows(matches, member) for member in values))


def deliver(payload):
    return lax.all_to_all(payload, ("rows", "grp"), split_axis=0, concat_axis=0, tiled=True)


def body(snap_early, snap_late, block_ids, block_owner, block_slot):
    members = lax.axis_size(("rows", "grp"))
    per_peer = (CAP + members - 1) // members
    row_total = snap_early.shape[0] * snap_early.shape[1] * members
    labels = jnp.arange(block_owner.shape[0], dtype=jnp.int32)
    hits = block_ids[:, None] == labels[None, :]
    owner_here = jnp.sum(jnp.where(hits, block_owner[None, :], 0), axis=1)
    slot_here = jnp.sum(jnp.where(hits, block_slot[None, :], 0), axis=1)
    destination = owner_here * per_peer + slot_here // members
    inverse, operator = finish(combine_stats(gram_pair(snap_early, snap_late)), row_total)
    payload = arrange(
        (apply_inverse(snap_late, inverse),), destination, slot_here, members * per_peer
    )
    arrived = deliver(payload)
    mode_blocks = settle(arrived[:1], arrived[1], CAP)[0]
    return (mode_blocks, operator)


def solution(mesh):
    placed = (
        P(("rows", "grp"), None, None),
        P(("rows", "grp"), None, None),
        P(("rows", "grp")),
        P(),
        P(),
    )
    return jax.shard_map(
        body,
        mesh=mesh,
        in_specs=placed,
        out_specs=(P(("rows", "grp"), None, None), P()),
        check_vma=False,
    )
```

profile of v0, /device:TPU:17, one launch (start us, length us, event | category | flops | bytes accessed | tf_op | source)
XLA Modules:
  0.0 743.5 jit_solution(3429416698145904338)
XLA Ops:
  0.7 13.4 %convolution_bitcast_fusion.4 = f32[1,128,128]{2,1,0:T(8,128)S(1)} fusion(f32[96,128,128]{2,1,0:T(8,128)} %param.9), kind=kOutput, calls=%fused_computation.35 | convolution fusion | flops 2415919104 | bytes 6356992 | tf_op jit(solution)/shard_map/rk,rl->kl/dot_general | solution.py:47
  14.1 10.0 %convolution_bitcast_fusion.3 = f32[1,128,128]{2,1,0:T(8,128)S(1)} fusion(f32[96,128,128]{2,1,0:T(8,128)S(1)} %copy-done, f32[96,128,128]{2,1,0:T(8,128)S(1)} %copy-done.1), kind=kOutput, calls=%fused_computation.34 | convolution fusion | flops 2415919104 | bytes 12648448 | tf_op jit(solution)/shard_map/rk,rl->kl/dot_general | solution.py:48
  24.9 1.0 collective-permute-done
  25.9 1.3 collective-permute-start.1
  27.6 3.1 collective-permute-done.1
  30.7 1.3 collective-permute-start.2
  32.0 2.6 collective-permute-done.2
  34.6 1.4 collective-permute-start.3
  36.2 2.3 collective-permute-done.3
  39.8 9.5 %all-to-all-start = ((s32[32,4,1]{1,2,0:T(1,128)}), s32[32,4,1]{1,2,0:T(1,128)S(1)}, u32[]{:S(2)}, u32[]{:S(2)}) async-start(s32[32,4,1]{1,2,0:T(1,128)} %bitcast), calls=%async_computation | async-start | bytes 32768 | tf_op jit(solution)/shard_map/all_to_all | solution.py:97
  49.4 229.2 %while.32 = (s32[]{:T(128)}, f32[128,128]{0,1:T(8,128)S(1)}, f32[128,128]{1,0:T(8,128)S(1)}, s32[]{:T(128)}, s32[]{:T(128)}) while((s32[]{:T(128)}, f32[128,128]{0,1:T(8,128)S(1)}, f32[128,128]{1,0:T(8,128)S(1)}, s32[]{:T(128)}, s32[]{:T(128)}) %tuple.86), condition=%wide.region_6.7_spmd.clone.clone, body=%wide.region_4.6_spmd.clone.clone.sunk | while | flops 263298 | bytes 333416 | solution.py:26
  53.0 0.9 fusion.60
  54.8 0.9 fusion.60
  58.3 0.9 fusion.60
  60.1 0.9 fusion.60
  63.7 0.9 fusion.60
  65.5 0.9 fusion.60
  69.1 0.9 fusion.60
  70.9 0.9 fusion.60
  74.5 0.9 fusion.60
  278.6 213.8 %while.31 = (s32[]{:T(128)}, f32[128,128]{1,0:T(8,128)S(1)}, f32[128,128]{1,0:T(8,128)S(1)}, s32[]{:T(128)}, s32[]{:T(128)}, /*index=5*/s32[]{:T(128)}, s32[]{:T(128)}) while((s32[]{:T(128)}, f32[128,128]{1,0:T(8,128)S(1)}, f32[128,128]{1,0:T(8,128)S(1)}, s32[]{:T(128)}, s32[]{:T(128)}, /*index=5*/s32[]{:T(128)}, s32[]{:T(128)}) %tuple.89), condition=%wide.region_9.10_spmd.clone, body=%wide.region_7.9_spmd.clone.sunk | while | flops 263302 | bytes 199850 | solution.py:41
  492.5 9.2 %convolution_bitcast_fusion.2 = f32[12288,128]{0,1:T(8,128)} fusion(f32[128,128]{1,0:T(8,128)S(1)} %get-tuple-element.195, f32[12288,128]{1,0:T(8,128)} %bitcast.73), kind=kOutput, calls=%fused_computation.25 | convolution fusion | flops 2415919104 | bytes 12648448 | tf_op jit(solution)/shard_map/dot_general | solution.py:70
  501.7 6.6 copy.31
  508.3 7.1 reshape_reshape.3
  515.4 6.1 fusion.18
  521.5 8.3 %copy.33 = f32[128,128,128]{2,1,0:T(8,128)} copy(f32[128,128,128]{2,0,1:T(8,128)S(1)} %fusion.18) | data formatting | bytes 16777216 | tf_op jit(solution)/shard_map/dot_general | solution.py:76
  529.8 6.3 all-to-all-start.1
  537.6 0.9 fusion.36
  538.5 179.8 %all-to-all-done.1 = f32[128,128,128]{2,1,0:T(8,128)} async-done(((f32[128,128,128]{2,1,0:T(8,128)}), f32[128,128,128]{2,1,0:T(8,128)}, u32[]{:S(2)}, u32[]{:S(2)}) %all-to-all-start.1) | async-done | bytes 8388640 | tf_op jit(solution)/shard_map/all_to_all | solution.py:97
  718.4 9.3 %copy.34 = f32[128,128,128]{0,2,1:T(8,128)} copy(f32[128,128,128]{2,1,0:T(8,128)} %all-to-all-done.1) | data formatting | bytes 16777216 | tf_op jit(solution)/shard_map/all_to_all | solution.py:97
  727.7 7.1 fusion.16
  734.8 8.3 %copy.35 = f32[128,128,128]{2,1,0:T(8,128)} copy(f32[128,128,128]{2,0,1:T(8,128)S(1)} %fusion.16) | data formatting | bytes 16777216
  (1177 shorter events, 334.0 us)
Async XLA Ops:
  0.6 13.4 %copy-start = (f32[96,128,128]{2,1,0:T(8,128)S(1)}, f32[96,128,128]{2,1,0:T(8,128)}, u32[]{:S(2)}) copy-start(f32[96,128,128]{2,1,0:T(8,128)} %param.9) | copy-start | bytes 18874372
  0.6 13.4 %copy-start.1 = (f32[96,128,128]{2,1,0:T(8,128)S(1)}, f32[96,128,128]{2,1,0:T(8,128)}, u32[]{:S(2)}) copy-start(f32[96,128,128]{2,1,0:T(8,128)} %param.10) | copy-start | bytes 18874372
  14.1 13.1 %copy-start.2 = (s32[3072]{0:T(1024)S(1)}, s32[3072]{0:T(1024)}, u32[]{:S(2)}) copy-start(s32[3072]{0:T(1024)} %param.12) | copy-start | bytes 36868
  14.1 13.1 %copy-start.3 = (s32[3072]{0:T(1024)S(1)}, s32[3072]{0:T(1024)}, u32[]{:S(2)}) copy-start(s32[3072]{0:T(1024)} %param.13) | copy-start | bytes 36868
  14.1 13.1 %copy-start.4 = (s32[96]{0:T(128)S(1)}, s32[96]{0:T(128)}, u32[]{:S(2)}) copy-start(s32[96]{0:T(128)} %param.11) | copy-start | bytes 1156
  24.2 1.7 collective-permute-start
  25.9 4.8 collective-permute-start.1
  30.7 3.9 collective-permute-start.2
  34.6 3.9 collective-permute-start.3
  38.5 10.8 %collective-permute-start.4 = (f32[2,128,128]{2,1,0:T(8,128)S(1)}, f32[2,128,128]{2,1,0:T(8,128)S(1)}, u32[]{:S(2)}, u32[]{:S(2)}) collective-permute-start(f32[2,128,128]{2,1,0:T(8,128)S(1)} %add.100), channel_id=1, source_target_pairs={{0,16},{1,17},{2,18},{3,19},{4,20},{5,21},{6,22},{7,23},{8,24},{9,... | collective-permute-start | bytes 393224 | tf_op jit(solution)/shard_map/ppermute | solution.py:10
  39.8 490.0 %all-to-all-start = ((s32[32,4,1]{1,2,0:T(1,128)}), s32[32,4,1]{1,2,0:T(1,128)S(1)}, u32[]{:S(2)}, u32[]{:S(2)}) async-start(s32[32,4,1]{1,2,0:T(1,128)} %bitcast), calls=%async_computation | async-start | bytes 32768 | tf_op jit(solution)/shard_map/all_to_all | solution.py:97
  529.8 188.6 %all-to-all-start.1 = ((f32[128,128,128]{2,1,0:T(8,128)}), f32[128,128,128]{2,1,0:T(8,128)}, u32[]{:S(2)}, u32[]{:S(2)}) async-start(f32[128,128,128]{2,1,0:T(8,128)} %copy.33), calls=%async_computation.1 | async-start | bytes 16777216 | tf_op jit(solution)/shard_map/all_to_all | solution.py:97
where the time goes:
time: 755 us; the launch traced here: 744 us
  matrix products  270 us (36%)
  waiting for transfers between devices  189 us (25%)
  other arithmetic  116 us (15%)
  loops' own time  105 us (14%)
  local copies, waits for them, and re-layouts  41 us (5%)
  starting transfers between devices  21 us (3%)
    all_to_all x2, waiting for transfers between devices, deliver(): lax.all_to_all(payload, ('rows', 'grp'), split_axis=0, concat_axis=0, til...  180 us
    dot_general x128, matrix products, step(): rest = grow - jnp.dot(column, factor, precision=lax.Precision.HIGHEST)  116 us
    dot_general x128, matrix products, step(): jnp.dot(frow, inverse, precision=lax.Precision.HIGHEST)  108 us
    another operation x1, loops' own time, upper_factor(): return lax.fori_loop(0, order, step, jnp.zeros_like(gram_total))  100 us
    reduce_sum x128, other arithmetic, step(): diagonal = jnp.sum(frow * unit)  87.9 us
    all_to_all x2, starting transfers between devices, deliver(): lax.all_to_all(payload, ('rows', 'grp'), split_axis=0, concat_axis=0, til...  15.8 us
  transfers between devices with their start and end apart: 7, of which 5 were waited for; matrix products, arithmetic and copies ran while one was open for 51% of the time, Pallas kernels for 0%

commit v1 on v0

v1 whole, which is shorter than its diff:
```python
import functools
import math

import jax
import jax.numpy as jnp
from jax import lax
from jax.experimental import pallas as pl
from jax.experimental.pallas import tpu as pltpu
from jax.sharding import PartitionSpec as P

CAP = 128
LANES = 128
TILE = 8
MESH = pl.DeviceIdType.MESH
HIGHEST = lax.Precision.HIGHEST


def arrange_kernel(place_ref, late_ref, payload_ref, sem):
    blocks = late_ref.shape[0]

    def send(i, carry):
        pltpu.make_async_copy(late_ref.at[i], payload_ref.at[place_ref[i]], sem).start()
        return carry

    lax.fori_loop(0, blocks, send, 0)
    pltpu.make_async_copy(late_ref, payload_ref.at[pl.ds(0, blocks)], sem).wait()


def arrange(place, late, slots):
    return pl.pallas_call(
        arrange_kernel,
        out_shape=jax.ShapeDtypeStruct((slots,) + late.shape[1:], late.dtype),
        in_specs=[
            pl.BlockSpec(memory_space=pltpu.SMEM),
            pl.BlockSpec(memory_space=pl.ANY),
        ],
        out_specs=pl.BlockSpec(memory_space=pl.ANY),
        scratch_shapes=[pltpu.SemaphoreType.DMA],
        compiler_params=pltpu.CompilerParams(has_side_effects=True),
    )(place, late)


def exchange_kernel(
    members, cores, per_peer, chunk, first, second, row_total,
    early_ref, late_ref, payload_ref, table_ref,
    arrived_ref, inverse_ref, operator_ref, slots_ref,
    early_buf, late_buf, stat, parts, summed, total, tables, work, left,
    in_sem, local_sem, table_send, table_recv, block_send, block_recv,
    part_send, part_recv, sum_send, sum_recv,
):
    me = lax.axis_index("rows") * cores + lax.axis_index("grp")
    order = stat.shape[1]
    share = parts.shape[1]
    reducers = stat.shape[0] // share
    half = members // 2

    def device(peer):
        return (lax.div(peer, cores), lax.rem(peer, cores))

    def table_copy(k):
        peer = me ^ k
        return pltpu.make_async_remote_copy(
            table_ref.at[peer], tables.at[me], table_send.at[k], table_recv.at[k],
            device_id=device(peer), device_id_type=MESH)

    def block_copy(k):
        peer = me ^ k
        return pltpu.make_async_remote_copy(
            payload_ref.at[pl.ds(peer * per_peer, per_peer)],
            arrived_ref.at[pl.ds(me * per_peer, per_peer)],
            block_send.at[k], block_recv.at[k],
            device_id=device(peer), device_id_type=MESH)

    def part_copy(k):
        peer = me ^ k
        return pltpu.make_async_remote_copy(
            stat.at[pl.ds(pl.multiple_of(peer * share, share), share)], parts.at[me],
            part_send.at[k], part_recv.at[k],
            device_id=device(peer), device_id_type=MESH)

    def sum_copy(k):
        return pltpu.make_async_remote_copy(
            summed, total.at[pl.ds(pl.multiple_of(me * share, share), share)],
            sum_send.at[k], sum_recv.at[k],
            device_id=device(me ^ k), device_id_type=MESH)

    def each(low, high, do):
        def step(k, carry):
            do(k)
            return carry
        lax.fori_loop(low, high, step, 0)

    def offset(i):
        return (i >> 1) + half * (1 - (i & 1))

    barrier = pltpu.get_barrier_semaphore()
    each(1, members, lambda k: pl.semaphore_signal(
        barrier, inc=1, device_id=device(me ^ k), device_id_type=MESH))

    own = pl.ds(me * per_peer, per_peer)
    own_blocks = pltpu.make_async_copy(payload_ref.at[own], arrived_ref.at[own], local_sem.at[0])
    own_blocks.start()
    own_table = pltpu.make_async_copy(table_ref.at[me], tables.at[me], local_sem.at[1])
    own_table.start()

    def loads(step, slot):
        rows = pl.ds(step * chunk, chunk)
        return (
            pltpu.make_async_copy(early_ref.at[rows], early_buf.at[slot], in_sem.at[slot, 0]),
            pltpu.make_async_copy(late_ref.at[rows], late_buf.at[slot], in_sem.at[slot, 1]),
        )

    for load in loads(0, 0):
        load.start()

    pl.semaphore_wait(barrier, members - 1)

    block_copy(half).start()
    each(2, first, lambda i: block_copy(offset(i)).start())
    each(1, members, lambda k: table_copy(k).start())

    stat[...] = jnp.zeros_like(stat)
    steps = early_ref.shape[0] // chunk

    def gram_step(step, carry):
        slot = step % 2

        @pl.when(step + 1 < steps)
        def _():
            for load in loads(step + 1, 1 - slot):
                load.start()

        for load in loads(step, slot):
            load.wait()
        early = early_buf[slot].reshape((-1, order))
        late = late_buf[slot].reshape((-1, order))
        contract = (((0,), (0,)), ((), ()))
        stat[0:order, :] += lax.dot_general(
            early, early, contract, precision=HIGHEST, preferred_element_type=jnp.float32)
        stat[order:2 * order, :] += lax.dot_general(
            early, late, contract, precision=HIGHEST, preferred_element_type=jnp.float32)
        return carry

    lax.fori_loop(0, steps, gram_step, 0)

    def to_reducers(k):
        @pl.when((me ^ k) < reducers)
        def _():
            part_copy(k).start()

    each(1, members, to_reducers)
    each(first, second, lambda i: block_copy(offset(i)).start())

    @pl.when(me < reducers)
    def _():
        mine = pl.ds(pl.multiple_of(me * share, share), share)
        parts[me] = stat[mine, :]
        each(1, members, lambda k: part_copy(k).wait_recv())
        summed[...] = jnp.sum(parts[...], axis=0) / row_total
        total[mine, :] = summed[...]
        each(1, members, lambda k: sum_copy(k).start())

    each(second, members, lambda i: block_copy(offset(i)).start())

    def from_reducers(k):
        @pl.when((me ^ k) < reducers)
        def _():
            part_copy(k).wait_send()
            sum_copy(k).wait_recv()

    each(1, members, from_reducers)

    work[...] = total[0:order, :]
    row_index = lax.broadcasted_iota(jnp.int32, (order, order), 0)
    lane_index = lax.broadcasted_iota(jnp.int32, (order, order), 1)
    left[...] = (row_index == lane_index).astype(jnp.float32)

    def eliminate(j, carry):
        square = work[...]
        row = work[pl.ds(j, 1), :]
        left_row = left[pl.ds(j, 1), :]
        picked = lane_index == j
        column = jnp.sum(jnp.where(picked, square, 0.0), axis=1, keepdims=True)
        pivot = jnp.sum(jnp.where(picked[0:1, :], row, 0.0), axis=1, keepdims=True)
        scale = jnp.where(row_index[:, 0:1] > j, column / pivot, 0.0)
        work[...] = square - scale * row
        left[...] = left[...] - scale * left_row
        return carry

    lax.fori_loop(0, order, eliminate, 0)
    diagonal = jnp.sum(jnp.where(row_index == lane_index, work[...], 0.0), axis=1, keepdims=True)
    lower = left[...] / jnp.sqrt(diagonal)
    inverse = lower.T
    inverse_ref[...] = inverse
    coupled = jnp.dot(total[order:2 * order, :], inverse, precision=HIGHEST, preferred_element_type=jnp.float32)
    operator_ref[...] = jnp.dot(lower, coupled, precision=HIGHEST, preferred_element_type=jnp.float32)

    @pl.when(me < reducers)
    def _():
        each(1, members, lambda k: sum_copy(k).wait_send())

    own_table.wait()
    each(1, members, lambda k: table_copy(k).wait())
    slots_ref[...] = jnp.sum(tables[...], axis=0).astype(jnp.int32)
    own_blocks.wait()
    each(1, members, lambda k: block_copy(k).wait())


def exchange(early, late, payload, table, members, cores, per_peer, row_total):
    order = early.shape[-1]
    chunk = math.gcd(early.shape[0], 8)
    share = max(TILE, 2 * order // members)
    first = max(2, members * 12 // 32)
    second = max(first, members * 22 // 32)
    sems = [pltpu.SemaphoreType.DMA((members,))] * 8
    vmem = pl.BlockSpec(memory_space=pltpu.VMEM)
    hbm = pl.BlockSpec(memory_space=pl.ANY)
    square = jax.ShapeDtypeStruct((order, order), jnp.float32)
    return pl.pallas_call(
        functools.partial(
            exchange_kernel, members, cores, per_peer, chunk, first, second, row_total),
        out_shape=[
            jax.ShapeDtypeStruct(payload.shape, payload.dtype),
            square,
            square,
            jax.ShapeDtypeStruct(table.shape[1:], jnp.int32),
        ],
        in_specs=[hbm, hbm, hbm, hbm],
        out_specs=[hbm, vmem, vmem, vmem],
        scratch_shapes=[
            pltpu.VMEM((2, chunk) + early.shape[1:], jnp.float32),
            pltpu.VMEM((2, chunk) + early.shape[1:], jnp.float32),
            pltpu.VMEM((2 * order, order), jnp.float32),
            pltpu.VMEM((members, share, order), jnp.float32),
            pltpu.VMEM((share, order), jnp.float32),
            pltpu.VMEM((2 * order, order), jnp.float32),
            pltpu.VMEM(table.shape, jnp.float32),
            pltpu.VMEM((order, order), jnp.float32),
            pltpu.VMEM((order, order), jnp.float32),
            pltpu.SemaphoreType.DMA((2, 2)),
            pltpu.SemaphoreType.DMA((2,)),
        ] + sems,
        compiler_params=pltpu.CompilerParams(
            collective_id=0, has_side_effects=True, vmem_limit_bytes=32 * 1024 * 1024),
    )(early, late, payload, table)


def settle_kernel(group, slots_ref, arrived_ref, inverse_ref, modes_ref, held, sems):
    step = pl.program_id(0)
    steps = pl.num_programs(0)

    @pl.when(step == 0)
    def _():
        def fetch(i, carry):
            index = jnp.maximum(slots_ref[0, i] - 1, 0)
            pltpu.make_async_copy(arrived_ref.at[index], held.at[i], sems.at[i // group]).start()
            return carry

        lax.fori_loop(0, steps * group, fetch, 0)

    mine = pl.ds(step * group, group)
    pltpu.make_async_copy(arrived_ref.at[pl.ds(0, group)], held.at[mine], sems.at[step]).wait()
    rows = held[mine].reshape((-1, held.shape[-1]))
    solved = jnp.dot(rows, inverse_ref[...], precision=HIGHEST, preferred_element_type=jnp.float32)
    solved = solved.reshape((group,) + held.shape[1:])
    for b in range(group):
        full = slots_ref[0, step * group + b] > 0
        modes_ref[b] = jnp.where(full, solved[b], 0.0)


def settle(slots, arrived, inverse):
    count = CAP
    group = 16
    block = arrived.shape[1:]
    return pl.pallas_call(
        functools.partial(settle_kernel, group),
        out_shape=jax.ShapeDtypeStruct((count,) + block, arrived.dtype),
        grid=(count // group,),
        in_specs=[
            pl.BlockSpec(memory_space=pltpu.SMEM),
            pl.BlockSpec(memory_space=pl.ANY),
            pl.BlockSpec(memory_space=pltpu.VMEM),
        ],
        out_specs=pl.BlockSpec((group,) + block, lambda s: (s, 0, 0)),
        scratch_shapes=[
            pltpu.VMEM((count,) + block, arrived.dtype),
            pltpu.SemaphoreType.DMA((count // group,)),
        ],
        compiler_params=pltpu.CompilerParams(vmem_limit_bytes=32 * 1024 * 1024),
    )(slots, arrived, inverse)


def body(snap_early, snap_late, block_ids, block_owner, block_slot):
    cores = lax.axis_size("grp")
    members = lax.axis_size(("rows", "grp"))
    per_peer = (CAP + members - 1) // members
    blocks = snap_early.shape[0]
    row_total = blocks * snap_early.shape[1] * members
    me = lax.axis_index(("rows", "grp"))
    labels = jnp.arange(block_owner.shape[0], dtype=jnp.int32)
    hits = block_ids[:, None] == labels[None, :]
    packed = block_owner * CAP + block_slot
    packed_here = jnp.sum(jnp.where(hits, packed[None, :], 0), axis=1)
    owner = packed_here // CAP
    slot = packed_here % CAP
    index = jnp.arange(blocks, dtype=jnp.int32)
    earlier = (owner[:, None] == owner[None, :]) & (index[None, :] < index[:, None])
    rank = jnp.sum(earlier.astype(jnp.int32), axis=1)
    place = owner * per_peer + rank
    peers = jnp.arange(members, dtype=jnp.int32)
    lanes = jnp.arange(LANES, dtype=jnp.int32)
    to_owner = (owner[None, :] == peers[:, None]).astype(jnp.float32)
    landing = (me * per_peer + rank + 1).astype(jnp.float32)
    at_slot = jnp.where(slot[:, None] == lanes[None, :], landing[:, None], 0.0)
    table = jnp.dot(to_owner, at_slot, precision=HIGHEST)
    table = jnp.pad(table[:, None, :], ((0, 0), (0, TILE - 1), (0, 0)))
    payload = arrange(place, snap_late, members * per_peer)
    arrived, inverse, operator, slots = exchange(
        snap_early, snap_late, payload, table, members, cores, per_peer, float(row_total))
    modes = settle(slots, arrived, inverse)
    return (modes, operator)


def solution(mesh):
    placed = (
        P(("rows", "grp"), None, None),
        P(("rows", "grp"), None, None),
        P(("rows", "grp")),
        P(),
        P(),
    )
    return jax.shard_map(
        body,
        mesh=mesh,
        in_specs=placed,
        out_specs=(P(("rows", "grp"), None, None), P()),
        check_vma=False,
    )
```

time: 755 us -> 428 us (0.57); the launches traced: 744 us -> 428 us
  Pallas kernels: 0 us -> 418 us
  matrix products: 270 us -> 0.2 us
  waiting for transfers between devices: 189 us -> 0 us
  other arithmetic: 116 us -> 2.38 us
  loops' own time: 105 us -> 0 us
  local copies, waits for them, and re-layouts: 41 us -> 6.24 us
  starting transfers between devices: 21 us -> 0 us
    pallas_call x0 -> x3, Pallas kernels: none -> 418 us  [the longest x1 204 us: exchange(): pl.pallas_call(functools.partial(exchange_kernel, members, cores, per_pee...]
    dot_general x263 -> x1, matrix products: 270 us -> 0.2 us  [body(): table = jnp.dot(to_owner, at_slot, precision=HIGHEST)]
    all_to_all x2 -> x0, waiting for transfers between devices: 180 us -> none  [deliver(): lax.all_to_all(payload, ('rows', 'grp'), split_axis=0, concat_axis=0, til...]
    another operation x2 -> x0, loops' own time: 105 us -> none  [the longest x1 100 us: upper_factor(): return lax.fori_loop(0, order, step, jnp.zeros_like(gram_total))]
    reduce_sum x130 -> x2, other arithmetic: 88.4 us -> 1.11 us  [the longest x1 0.94 us: body(): packed_here = jnp.sum(jnp.where(hits, packed[None, :], 0), axis=1)]
    add x262 -> x1, other arithmetic: 23.8 us -> 0.73 us  [body(): packed = block_owner * CAP + block_slot]
    all_to_all x2 -> x0, starting transfers between devices: 15.8 us -> none  [deliver(): lax.all_to_all(payload, ('rows', 'grp'), split_axis=0, concat_axis=0, til...]
    dot_general x2 -> x0, local copies, waits for them, and re-layouts: 14.8 us -> none  [the longest x1 8.25 us: select_rows(): jnp.dot(matches.astype(member.dtype), flat, precision=lax.Precision.HIGHEST)]
  transfers between devices with their start and end apart: 7 -> 0, of which waited for: 5 -> 0; matrix products, arithmetic and copies ran while one was open for 51% -> 0% of each run, Pallas kernels for 0% -> 0%
where the time goes in v1:
time: 428 us
  Pallas kernels  418 us (98%)
  local copies, waits for them, and re-layouts  6.24 us (1%)
    pallas_call x1, Pallas kernels, exchange(): pl.pallas_call(functools.partial(exchange_kernel, members, cores, per_pee...  204 us
    pallas_call x1, Pallas kernels, arrange(): pl.pallas_call(arrange_kernel, out_shape=jax.ShapeDtypeStruct((slots,) +...  192 us
    pallas_call x1, Pallas kernels, settle(): pl.pallas_call(functools.partial(settle_kernel, group), out_shape=jax.Sha...  21.9 us

profile of v1, /device:TPU:17, one launch (start us, length us, event | category | flops | bytes accessed | tf_op | source)
XLA Modules:
  0.0 427.7 jit_solution(4962750774078667095)
XLA Ops:
  0.6 0.7 multiply_add_fusion
  1.4 0.9 select_reduce_fusion
  2.3 0.2 convert_reduce_fusion
  2.5 0.5 add_convert_fusion
  3.0 0.2 fusion
  3.3 192.4 %shard_map.68.payload_ref = f32[128,128,128]{2,1,0:T(8,128)} custom-call(s32[96]{0:T(128)} %get-tuple-element.13.place_ref, f32[96,128,128]{2,1,0:T(8,128)} %late_ref.3), custom_call_target="tpu_custom_call" | custom-call | tf_op jit(solution)/shard_map/pallas_call | solution.py:30
  195.7 0.0 copy-start
  195.7 2.8 copy-done
  198.4 0.0 copy-start.1
  198.4 2.8 copy-done.1
  201.2 203.9 %shard_map.69 = (f32[128,128,128]{2,1,0:T(8,128)S(1)}, f32[128,128]{1,0:T(8,128)S(1)}, f32[128,128]{1,0:T(8,128)S(1)}, s32[8,128]{1,0:T(8,128)S(1)}) custom-call(f32[96,128,128]{2,1,0:T(8,128)S(1)} %copy-done.1, f32[96,128,128]{2,1,0:T(8,128)S(1)} %copy-done, f32[128,128,128]{2,1,0:T(8,128)} %shard_map.68.payload_ref, f32[32,8,128]{2,1,0:T(8,128)S(1)} %pad.4.table_ref), custom_call_target="tpu_custom_call" | custom-call | tf_op jit(solution)/shard_map/pallas_call | solution.py:219
  405.1 21.9 %shard_map.70 = f32[128,128,128]{2,1,0:T(8,128)} custom-call(s32[8,128]{1,0:T(8,128)S(1)} %get-tuple-element.6.slots_ref, f32[128,128,128]{2,1,0:T(8,128)S(1)} %get-tuple-element.7.arrived_ref, f32[128,128]{1,0:T(8,128)S(1)} %get-tuple-element.8.inverse_ref), custom_call_target="tpu_custom_call" | custom-call | tf_op jit(solution)/shard_map/pallas_call | solution.py:275
  427.1 0.6 copy.8
  (2 shorter events, 0.1 us)
Async XLA Ops:
  195.7 2.8 copy-start
  198.4 2.8 copy-start.1
